TPU v7x, 32 devices: a whole 2x2x4 slice. The times are simulated.
32 devices in a mesh: dp: 8 (over z, x), seq: 4 (over y, core).
Axes of the slice: x: 2, y: 2, z: 4, core: 2. Of those that a mesh axis runs over, the one named last changes fastest.
Arguments:
- output_gradient: bfloat16 [6144, 8192], P('dp'), may hold values from -6 to 6
- frozen_down_weight: bfloat16 [14336, 8192], P('seq', 'dp'), may hold values from -0.046875 to 0.046875
- adapter_first_factor: bfloat16 [14336, 64], P('seq'), may hold values from -0.046875 to 0.046875
- adapter_second_factor: bfloat16 [64, 8192], replicated, may hold values from -0.0625 to 0.0625
- kept_hidden_rows: bfloat16 [1536, 14336], P('dp', 'seq'), may hold values from -6 to 6
- kept_row_index: int32 [1536], P('dp'), may hold values from 0 to 767, as said below
- kept_row_count: int32 [8], P('dp'), may hold values from 1 to 192, 768 in all
- kept_row_scale: float32 [1536], P('dp'), may hold values from 1 to 8
Outputs:
- hidden_gradient: bfloat16 [6144, 14336], P('dp', 'seq')
- first_factor_gradient: float32 [14336, 64], P('seq')
- second_factor_gradient: float32 [64, 8192], P(None, ('dp', 'seq'))
Inputs may be any that keep to these rules, and one draw needn't show every extreme that they name: `kept_row_index`: within each aligned block of 192 entries (one dp index) the entries are distinct; only the first kept_row_count entries of a block are valid.
All inputs are finite; a program needn't handle non-finite values. No bound on the sum of `kept_row_count` on one device may be relied on, other than what follows from the above.
Results may differ from a plain program's by a relative error of at most 0.0051.
Values may be sent and summed in bfloat16 or wider, within the bound.
A program may use at most 192 MiB of HBM per device.

v0:
```python
import jax
import jax.numpy as jnp
from jax import lax
from jax.sharding import PartitionSpec as P

adapter_scale = 2.0


def on_device(
    output_gradient,
    frozen_down_weight,
    adapter_first_factor,
    adapter_second_factor,
    kept_hidden_rows,
    kept_row_index,
    kept_row_count,
    kept_row_scale,
):
    contract_dims = (((1,), (1,)), ((), ()))
    first_factor_out = (((0,), (0,)), ((), ()))
    token_rows = output_gradient.shape[0]
    frozen_product = lax.dot_general(
        output_gradient,
        lax.all_gather(frozen_down_weight, "dp", axis=1, tiled=True),
        contract_dims,
        preferred_element_type=jnp.float32,
    )
    adapter_gradient = lax.dot_general(
        output_gradient, adapter_second_factor, contract_dims, preferred_element_type=jnp.float32
    ).astype(jnp.bfloat16)
    adapter_contribution = lax.dot_general(
        adapter_gradient, adapter_first_factor, contract_dims, preferred_element_type=jnp.float32
    )
    hidden_gradient = (frozen_product + adapter_scale * adapter_contribution).astype(jnp.bfloat16)
    slots = kept_row_index.shape[0]
    valid = (jnp.arange(slots, dtype=jnp.int32) < kept_row_count[0]).astype(jnp.float32)
    weight_rows = kept_row_scale * valid
    gradient_kept_rows = jnp.take(adapter_gradient, kept_row_index, axis=0)
    w_rows = (weight_rows[:, None] * gradient_kept_rows.astype(jnp.float32)).astype(jnp.bfloat16)
    part_a = lax.dot_general(
        kept_hidden_rows, w_rows, first_factor_out, preferred_element_type=jnp.float32
    ) * (adapter_scale / token_rows)
    first_factor_gradient = lax.psum(part_a, "dp")
    output_gradient_kept = jnp.take(output_gradient, kept_row_index, axis=0)
    partial_hidden_gradient = jnp.dot(
        kept_hidden_rows, adapter_first_factor, preferred_element_type=jnp.float32
    )
    scaled_gradient_rows = weight_rows[:, None] * partial_hidden_gradient
    chosen = output_gradient_kept.astype(jnp.float32)
    term_b = lax.dot_general(
        scaled_gradient_rows,
        chosen,
        first_factor_out,
        precision=lax.Precision.HIGHEST,
        preferred_element_type=jnp.float32,
    ) * (adapter_scale / token_rows)
    second_factor_gradient = lax.psum_scatter(
        term_b, ("dp", "seq"), scatter_dimension=1, tiled=True
    )
    return (hidden_gradient, first_factor_gradient, second_factor_gradient)


def solution(mesh):
    in_specs = (
        P("dp", None),
        P("seq", "dp"),
        P("seq", None),
        P(),
        P("dp", "seq"),
        P("dp"),
        P("dp"),
        P("dp"),
    )
    out_specs = (P("dp", "seq"), P("seq", None), P(None, ("dp", "seq")))
    return jax.shard_map(
        on_device, mesh=mesh, in_specs=in_specs, out_specs=out_specs, check_vma=False
    )
```

profile of v0, /device:TPU:0, one launch (start us, length us, event | category | flops | bytes accessed | tf_op | source)
XLA Modules:
  0.0 1239.8 jit_solution(10007248082175373315)
XLA Ops:
  8.0 0.0 copy-start
  8.0 0.0 copy-start.3
  8.0 0.0 all-gather.2.cloned.1.call-start
  8.1 0.7 all-gather.2.cloned.1.call-update
  8.8 0.0 copy-start.4
  8.8 0.0 copy-start.5
  8.8 0.0 all-reduce.2.cloned.1.call-start
  8.8 0.5 copy-done.3
  9.3 8.5 convolution_convert_fusion
  17.8 0.2 copy.11
  18.7 0.0 copy-done.4
  18.7 0.8 gather_fusion
  19.5 0.0 copy-done.5
  19.5 0.0 copy-done
  19.5 1.4 fusion
  21.0 0.0 all-reduce.2.cloned.1.call-update
  21.0 0.0 copy-start.2
  21.0 0.2 reduce-scatter.2.cloned.1.call-start
  21.2 14.4 %gather_fusion.1 = bf16[192,8192]{1,0:T(8,128)(2,1)} fusion(bf16[768,8192]{1,0:T(8,128)(2,1)} %param.8, s32[1024]{0:T(1024)S(1)} %pad_clamp_fusion), kind=kCustom, calls=%fused_computation.1 | custom fusion | bytes 6292224 | tf_op jit(solution)/shard_map/jit(_take)/gather | solution.py:44
  35.7 0.0 copy-done.2
  35.7 0.5 convolution_multiply_fusion.2
  36.2 5.1 convolution_multiply_fusion
  41.3 0.0 reduce-scatter.2.cloned.1.call-update
  41.4 1083.9 %all-gather.2.cloned.1.call-done = bf16[3584,8192]{1,0:T(8,128)(2,1)} async-done(((bf16[3584,1024]{1,0:T(8,128)(2,1)}), bf16[3584,8192]{1,0:T(8,128)(2,1)}) %all-gather.2.cloned.1.call-update) | async-done | bytes 58720272 | tf_op jit(solution)/shard_map/all_gather | solution.py:24
  1125.2 0.0 copy-start.1
  1125.2 55.2 %fusion.10 = f32[768,3584]{1,0:T(8,128)} fusion(bf16[768,8192]{1,0:T(8,128)(2,1)} %param.8, bf16[3584,8192]{1,0:T(8,128)(2,1)} %all-gather.2.cloned.1.call-done), kind=kOutput, calls=%fused_computation.22 | convolution fusion | flops 45097156608 | bytes 82313216 | tf_op jit(solution)/shard_map/dot_general | solution.py:22
  1180.4 8.2 add_convert_fusion
  1188.6 41.6 %all-reduce.2.cloned.1.call-done = f32[3584,64]{0,1:T(8,128)} async-done(((f32[3584,64]{0,1:T(8,128)}), f32[3584,64]{0,1:T(8,128)}) %all-reduce.2.cloned.1.call-update) | async-done | bytes 917520 | tf_op jit(solution)/shard_map/psum | solution.py:43
  1230.2 0.0 reduce-scatter.2.cloned.1.call-done
  1230.2 2.2 copy.14
  1232.3 0.0 copy-done.1
  (4 shorter events, 0.0 us)
Async XLA Ops:
  8.0 11.5 copy-start
  8.0 1.3 copy-start.3
  8.0 1117.2 %all-gather.2.cloned.1.call-start = ((), (), s32[]{:S(2)}) async-start(), calls=%async_computation.1 | async-start | bytes 66060288 | tf_op jit(solution)/shard_map/all_gather | solution.py:24
  8.8 9.9 copy-start.4
  8.8 10.8 copy-start.5
  8.8 1221.4 %all-reduce.2.cloned.1.call-start = ((), (), s32[]{:S(2)}) async-start(), calls=%async_computation.2 | async-start | bytes 1835008 | tf_op jit(solution)/shard_map/psum | solution.py:43
  21.0 14.7 %copy-start.2 = (bf16[3584,64]{0,1:T(8,128)(2,1)S(1)}, bf16[3584,64]{0,1:T(8,128)(2,1)}, u32[]{:S(2)}) copy-start(bf16[3584,64]{0,1:T(8,128)(2,1)} %param.10) | copy-start | bytes 1376260
  21.0 1209.1 %reduce-scatter.2.cloned.1.call-start = ((), (), s32[]{:S(2)}) async-start(), calls=%async_computation.3 | async-start | bytes 2162688 | tf_op jit(solution)/shard_map/reduce_scatter | solution.py:57
  1125.2 107.1 %copy-start.1 = (bf16[192,3584]{1,0:T(8,128)(2,1)S(1)}, bf16[192,3584]{1,0:T(8,128)(2,1)}, u32[]{:S(2)}) copy-start(bf16[192,3584]{1,0:T(8,128)(2,1)} %param.12) | copy-start | bytes 4128772
Sparse Core Ops, SparseCore 0:
  10.4 1114.7 all-gather.1
  1129.3 100.8 all-reduce.1
Sparse Core Ops, SparseCore 1:
  41.4 1185.5 reduce-scatter.1
where the time goes:
time: 1240 us
  waiting for transfers between devices  1130 us (91%)
  matrix products  78.9 us (6%)
  local copies, waits for them, and re-layouts  18.1 us (1%)
  between operations  16.2 us (1%)
    all_gather x1, waiting for transfers between devices, on_device(): lax.all_gather(frozen_down_weight, 'dp', axis=1, tiled=True)  1080 us
    dot_general x1, matrix products, on_device(): lax.dot_general(output_gradient, lax.all_gather(frozen_down_weight, 'dp',...  55.2 us
    psum x1, waiting for transfers between devices, on_device(): first_factor_gradient = lax.psum(part_a, 'dp')  41.6 us
  transfers between devices with their start and end apart: 3, of which 2 were waited for; matrix products, arithmetic and copies ran while one was open for 8% of the time, Pallas kernels for 0%

commit v1 on v0

--- a/solution.py
+++ b/solution.py
@@ -1,12 +1,240 @@
+import functools
+
 import jax
 import jax.numpy as jnp
 from jax import lax
+from jax.experimental import pallas as pl
+from jax.experimental.pallas import tpu as pltpu
 from jax.sharding import PartitionSpec as P
 
 adapter_scale = 2.0
+MESH = pl.DeviceIdType.MESH
+GROUP = 4
+AHEAD = 8
+RELAY = 4
+LAG = 4
+BUFS = 4
+
+
+def nt(a, b):
+    return lax.dot_general(a, b, (((1,), (1,)), ((), ())), preferred_element_type=jnp.float32)
+
+
+def hidden_kernel(
+    n_rs, n_seq, tile, og, w, lora_g, first, out,
+    slots, acts, part_in, part_out, staged,
+    s1s, s1r, s2s, s2r, s3s, s3r, pss, psr, axs, axr, bcs, bcr, loc, outs,
+):
+    d, s = lax.axis_index("dp"), lax.axis_index("seq")
+    hi, lo = d // GROUP, lax.rem(d, GROUP)
+    chunks = w.shape[0] // tile
+    width = w.shape[1]
+    tokens = og.shape[0]
+    quarter = tokens // n_seq
+
+    def xor(value, bits):
+        result = value
+        step = 1
+        while step <= bits:
+            if bits & step:
+                result = result + step - 2 * step * lax.rem(result // step, 2)
+            step *= 2
+        return result
+
+    px, pz = (xor(d, 1), s), (xor(d, 2), s)
+    partners = [(xor(hi, r) * GROUP + lo, s) for r in range(1, n_rs)]
+    peers = [(d, xor(s, q)) for q in range(1, n_seq)]
+
+    barrier = pltpu.get_barrier_semaphore()
+    for other in [px, pz] + partners + peers:
+        pl.semaphore_signal(barrier, inc=1, device_id=other, device_id_type=MESH)
+    pl.semaphore_wait(barrier, 2 + len(partners) + len(peers))
+
+    def rows(c):
+        return pl.ds(pl.multiple_of(c * tile, tile), tile)
+
+    def remote(src, dst, send, recv, device):
+        return pltpu.make_async_remote_copy(
+            src_ref=src, dst_ref=dst, send_sem=send, recv_sem=recv,
+            device_id=device, device_id_type=MESH,
+        )
+
+    def own_x(c):
+        return remote(w.at[rows(c)], slots.at[1, rows(c)], s1s.at[c], s1r.at[c], px)
+
+    def own_z(c):
+        return remote(w.at[rows(c)], slots.at[2, rows(c)], s2s.at[c], s2r.at[c], pz)
+
+    def relay(c):
+        return remote(slots.at[2, rows(c)], slots.at[3, rows(c)], s3s.at[c], s3r.at[c], px)
+
+    def partial(r, c):
+        return remote(
+            part_out.at[r, lax.rem(c, BUFS)], part_in.at[r, c], pss.at[r, c], psr.at[r, c], partners[r]
+        )
+
+    my_rows = pl.ds(pl.multiple_of(s * quarter, quarter), quarter)
+
+    def columns(group, j):
+        return pl.ds(pl.multiple_of((group * GROUP + xor(lo, j)) * width, width), width)
+
+    def exchange(r, j):
+        return remote(
+            og.at[my_rows, columns(xor(hi, r + 1), j)], acts.at[r + 1, j, my_rows],
+            axs.at[r, j], axr.at[r, j], partners[r],
+        )
+
+    def spread(r, j, q):
+        return remote(
+            acts.at[r + 1, j, my_rows], acts.at[r + 1, j, my_rows],
+            bcs.at[r, j, q], bcr.at[r, j, q], peers[q],
+        )
+
+    local = [pltpu.make_async_copy(w, slots.at[0], loc.at[GROUP])]
+    for j in range(GROUP):
+        local.append(pltpu.make_async_copy(og.at[:, columns(hi, j)], acts.at[0, j], loc.at[j]))
+
+    for j in range(GROUP):
+        for r in range(n_rs - 1):
+            exchange(r, j).start()
+    ahead = min(AHEAD, chunks)
+    relayed = min(RELAY, chunks)
+
+    @pl.loop(0, ahead)
+    def _(c):
+        own_z(c).start()
+        own_x(c).start()
+
+    for copy in local:
+        copy.start()
+    for j in range(GROUP):
+        for r in range(n_rs - 1):
+            exchange(r, j).wait_recv()
+            for q in range(n_seq - 1):
+                spread(r, j, q).start()
+        if j < relayed:
+            own_z(j).wait_recv()
+            relay(j).start()
+    for copy in local:
+        copy.wait()
+    for j in range(GROUP):
+        for r in range(n_rs - 1):
+            for q in range(n_seq - 1):
+                spread(r, j, q).wait_recv()
+
+    def product(b, c):
+        total = nt(acts[b, 0], slots[0, rows(c)])
+        for j in range(1, GROUP):
+            total += nt(acts[b, j], slots[j, rows(c)])
+        return total
+
+    def store(c):
+        at = lax.rem(c, 2)
+        return pltpu.make_async_copy(
+            staged.at[at], out.at[:, rows(c)], outs.at[at]
+        )
+
+    lag = min(LAG, chunks)
+
+    @pl.loop(0, chunks + lag)
+    def _(c):
+        @pl.when(c + ahead < chunks)
+        def _():
+            own_z(c + ahead).start()
+            own_x(c + ahead).start()
+
+        @pl.when(c + relayed < chunks)
+        def _():
+            own_z(c + relayed).wait_recv()
+            relay(c + relayed).start()
+
+        @pl.when(c < chunks)
+        def _():
+            own_x(c).wait_recv()
+            relay(c).wait_recv()
+            for r in range(n_rs - 1):
+                @pl.when(c >= BUFS)
+                def _():
+                    partial(r, c - BUFS).wait_send()
+                part_out[r, lax.rem(c, BUFS)] = product(r + 1, c).astype(jnp.bfloat16)
+                partial(r, c).start()
+
+        @pl.when(c >= lag)
+        def _():
+            f = c - lag
+            total = product(0, f) + adapter_scale * nt(lora_g[...], first[rows(f)])
+            for r in range(n_rs - 1):
+                partial(r, f).wait_recv()
+                total += part_in[r, f].astype(jnp.float32)
+
+            @pl.when(f >= 2)
+            def _():
+                store(f - 2).wait()
+            staged[lax.rem(f, 2)] = total.astype(jnp.bfloat16)
+            store(f).start()
+
+    for f in range(max(chunks - 2, 0), chunks):
+        store(f).wait()
+
+    @pl.loop(0, chunks)
+    def _(c):
+        own_x(c).wait_send()
+        own_z(c).wait_send()
+        relay(c).wait_send()
+
+    for r in range(n_rs - 1):
+        for f in range(max(chunks - BUFS, 0), chunks):
+            partial(r, f).wait_send()
+        for j in range(GROUP):
+            exchange(r, j).wait_send()
+            for q in range(n_seq - 1):
+                spread(r, j, q).wait_send()
+
+
+def hidden(n_dp, n_seq, og, w, lora_g, first):
+    tokens, hidden_rows, width = og.shape[0], w.shape[0], w.shape[1]
+    n_rs = n_dp // GROUP
+    tile = next(t for t in (256, 128) if hidden_rows % t == 0)
+    chunks = hidden_rows // tile
+    dma = pltpu.SemaphoreType.DMA
+    bf16 = jnp.bfloat16
+    others = n_rs - 1
+    return pl.pallas_call(
+        functools.partial(hidden_kernel, n_rs, n_seq, tile),
+        out_shape=jax.ShapeDtypeStruct((tokens, hidden_rows), bf16),
+        in_specs=[
+            pl.BlockSpec(memory_space=pl.ANY),
+            pl.BlockSpec(memory_space=pl.ANY),
+            pl.BlockSpec(memory_space=pltpu.VMEM),
+            pl.BlockSpec(memory_space=pltpu.VMEM),
+        ],
+        out_specs=pl.BlockSpec(memory_space=pl.ANY),
+        scratch_shapes=[
+            pltpu.VMEM((GROUP, hidden_rows, width), bf16),
+            pltpu.VMEM((n_rs, GROUP, tokens, width), bf16),
+            pltpu.VMEM((others, chunks, tokens, tile), bf16),
+            pltpu.VMEM((others, BUFS, tokens, tile), bf16),
+            pltpu.VMEM((2, tokens, tile), bf16),
+            dma((chunks,)), dma((chunks,)), dma((chunks,)),
+            dma((chunks,)), dma((chunks,)), dma((chunks,)),
+            dma((others, chunks)), dma((others, chunks)),
+            dma((others, GROUP)), dma((others, GROUP)),
+            dma((others, GROUP, n_seq - 1)), dma((others, GROUP, n_seq - 1)),
+            dma((GROUP + 1,)), dma((2,)),
+        ],
+        compiler_params=pltpu.CompilerParams(
+            collective_id=0, has_side_effects=True, vmem_limit_bytes=62 * 1024 * 1024
+        ),
+        cost_estimate=pl.CostEstimate(
+            flops=2 * tokens * hidden_rows * width * n_dp,
+            bytes_accessed=og.size * 2 + w.size * 2 * GROUP, transcendentals=0,
+        ),
+    )(og, w, lora_g, first)
 
 
 def on_device(
+    n_dp,
+    n_seq,
     output_gradient,
     frozen_down_weight,
     adapter_first_factor,
@@ -19,19 +247,12 @@
     contract_dims = (((1,), (1,)), ((), ()))
     first_factor_out = (((0,), (0,)), ((), ()))
     token_rows = output_gradient.shape[0]
-    frozen_product = lax.dot_general(
-        output_gradient,
-        lax.all_gather(frozen_down_weight, "dp", axis=1, tiled=True),
-        contract_dims,
-        preferred_element_type=jnp.float32,
-    )
     adapter_gradient = lax.dot_general(
         output_gradient, adapter_second_factor, contract_dims, preferred_element_type=jnp.float32
     ).astype(jnp.bfloat16)
-    adapter_contribution = lax.dot_general(
-        adapter_gradient, adapter_first_factor, contract_dims, preferred_element_type=jnp.float32
-    )
-    hidden_gradient = (frozen_product + adapter_scale * adapter_contribution).astype(jnp.bfloat16)
+    hidden_gradient = hidden(
+        n_dp, n_seq, output_gradient, frozen_down_weight, adapter_gradient, adapter_first_factor
+    )
     slots = kept_row_index.shape[0]
     valid = (jnp.arange(slots, dtype=jnp.int32) < kept_row_count[0]).astype(jnp.float32)
     weight_rows = kept_row_scale * valid
@@ -73,5 +294,6 @@
     )
     out_specs = (P("dp", "seq"), P("seq", None), P(None, ("dp", "seq")))
     return jax.shard_map(
-        on_device, mesh=mesh, in_specs=in_specs, out_specs=out_specs, check_vma=False
-    )
+        functools.partial(on_device, mesh.shape["dp"], mesh.shape["seq"]),
+        mesh=mesh, in_specs=in_specs, out_specs=out_specs, check_vma=False
+    )

time: 1240 us -> 452 us (0.36)
  waiting for transfers between devices: 1130 us -> 0.08 us
  Pallas kernels: 0 us -> 397 us
  matrix products: 78.9 us -> 15.4 us
    all_gather x1 -> x0, waiting for transfers between devices: 1080 us -> none  [on_device(): lax.all_gather(frozen_down_weight, 'dp', axis=1, tiled=True)]
    pallas_call x0 -> x1, Pallas kernels: none -> 397 us  [hidden(): pl.pallas_call(functools.partial(hidden_kernel, n_rs, n_seq, tile), out_s...]
    dot_general x2 -> x0, matrix products: 63.4 us -> none  [the longest x1 55.2 us: on_device(): lax.dot_general(output_gradient, lax.all_gather(frozen_down_weight, 'dp',...]
    psum x1, waiting for transfers between devices: 41.6 us -> 0.02 us  [on_device(): first_factor_gradient = lax.psum(part_a, 'dp')]
  transfers between devices with their start and end apart: 3 -> 2, of which waited for: 2 -> 0; matrix products, arithmetic and copies ran while one was open for 8% -> 4% of each run, Pallas kernels for 0% -> 88%
where the time goes in v1:
time: 452 us
  Pallas kernels  397 us (88%)
  local copies, waits for them, and re-layouts  21.6 us (5%)
  between operations  16.2 us (4%)
  matrix products  15.4 us (3%)
    pallas_call x1, Pallas kernels, hidden(): pl.pallas_call(functools.partial(hidden_kernel, n_rs, n_seq, tile), out_s...  397 us
    gather x1, local copies, waits for them, and re-layouts, on_device(): output_gradient_kept = jnp.take(output_gradient, kept_row_index, axis=0)  13.2 us
  transfers between devices with their start and end apart: 2, of which 0 were waited for; matrix products, arithmetic and copies ran while one was open for 4% of the time, Pallas kernels for 88%

profile of v1, /device:TPU:0, one launch (start us, length us, event | category | flops | bytes accessed | tf_op | source)
XLA Modules:
  0.0 452.2 jit_solution(16662711312430550748)
XLA Ops:
  8.0 0.0 copy-start
  8.0 0.0 all-reduce.2.cloned.1.call-start
  8.1 0.8 compare_select_fusion
  8.8 0.7 compare_and_fusion
  10.2 0.0 copy-start.4
  10.2 8.2 %convolution_convert_fusion.lora_g = bf16[768,64]{1,0:T(8,128)(2,1)S(1)} fusion(bf16[768,8192]{1,0:T(8,128)(2,1)} %og.1, bf16[64,8192]{1,0:T(8,128)(2,1)} %param.11), kind=kOutput, calls=%fused_computation.8 | convolution fusion | flops 805355520 | bytes 13729792 | tf_op jit(solution)/shard_map/dot_general | solution.py:250
  18.4 0.0 copy-start.3
  18.4 0.8 gather_fusion
  19.2 0.0 copy-done.4
  19.2 0.0 copy-done
  19.2 1.5 fusion
  20.7 0.0 all-reduce.2.cloned.1.call-update
  20.8 0.0 copy-start.1
  20.8 0.2 reduce-scatter.2.cloned.1.call-start
  21.0 13.2 %gather_fusion.1 = bf16[192,8192]{1,0:T(8,128)(2,1)} fusion(bf16[768,8192]{1,0:T(8,128)(2,1)} %og.1, s32[1024]{0:T(1024)S(1)} %pad_clamp_fusion), kind=kCustom, calls=%fused_computation.1 | custom fusion | bytes 6292224 | tf_op jit(solution)/shard_map/jit(_take)/gather | solution.py:265
  34.2 0.0 copy-done.3
  34.2 0.0 copy-done.1
  34.2 0.5 convolution_multiply_fusion.2
  34.7 5.2 %convolution_multiply_fusion = f32[64,8192]{1,0:T(8,128)} fusion(f32[192,64]{1,0:T(8,128)S(1)} %convolution_multiply_fusion.2, bf16[192,8192]{1,0:T(8,128)(2,1)} %gather_fusion.1, pred[192]{0:T(512)(128)(4,1)S(1)} %compare_and_fusion), kind=kOutput, calls=%fused_computation.2 | convolution fusion | flops 1210056704 | bytes 5292224 | tf_op jit(solution)/shard_map/dot_general | solution.py:271
  39.9 0.0 reduce-scatter.2.cloned.1.call-update
  39.9 1.2 copy.12.first
  41.2 397.2 %shard_map.103 = bf16[768,3584]{1,0:T(8,128)(2,1)} custom-call(bf16[768,8192]{1,0:T(8,128)(2,1)} %og.1, bf16[3584,1024]{1,0:T(8,128)(2,1)} %w.1, bf16[768,64]{1,0:T(8,128)(2,1)} %copy-done.3, bf16[3584,64]{1,0:T(8,128)(2,1)} %copy.12.first), custom_call_target="tpu_custom_call" | custom-call | flops 45097156608 | bytes 41943040 | tf_op jit(solution)/shard_map/pallas_call | solution.py:202
  438.3 0.0 all-reduce.2.cloned.1.call-done
  438.4 0.0 copy-start.2
  438.4 0.0 reduce-scatter.2.cloned.1.call-done
  438.4 5.4 %copy.17 = bf16[768,3584]{1,0:T(8,128)(2,1)} copy(bf16[768,3584]{1,0:T(8,128)(2,1)} %shard_map.103) | data formatting | bytes 11010048
  443.8 0.0 copy-done.2
  443.8 0.9 copy.18
  (2 shorter events, 0.0 us)
Async XLA Ops:
  8.0 11.2 %copy-start = (bf16[192,3584]{1,0:T(8,128)(2,1)S(1)}, bf16[192,3584]{1,0:T(8,128)(2,1)}, u32[]{:S(2)}) copy-start(bf16[192,3584]{1,0:T(8,128)(2,1)} %param.12) | copy-start | bytes 4128772
  8.0 430.3 %all-reduce.2.cloned.1.call-start = ((), (), s32[]{:S(2)}) async-start(), calls=%async_computation.1 | async-start | bytes 1835008 | tf_op jit(solution)/shard_map/psum | solution.py:264
  10.2 9.0 %copy-start.4 = (f32[192]{0:T(256)S(1)}, f32[192]{0:T(256)}, u32[]{:S(2)}) copy-start(f32[192]{0:T(256)} %param.15) | copy-start | bytes 2308
  18.4 15.8 %copy-start.3 = (bf16[768,64]{1,0:T(8,128)(2,1)}, bf16[768,64]{1,0:T(8,128)(2,1)S(1)}, u32[]{:S(2)}) copy-start(bf16[768,64]{1,0:T(8,128)(2,1)S(1)} %convolution_convert_fusion.lora_g) | copy-start | bytes 294916
  20.8 13.5 %copy-start.1 = (bf16[3584,64]{0,1:T(8,128)(2,1)S(1)}, bf16[3584,64]{0,1:T(8,128)(2,1)}, u32[]{:S(2)}) copy-start(bf16[3584,64]{0,1:T(8,128)(2,1)} %param.10) | copy-start | bytes 1376260
  20.8 417.6 %reduce-scatter.2.cloned.1.call-start = ((), (), s32[]{:S(2)}) async-start(), calls=%async_computation.2 | async-start | bytes 2162688 | tf_op jit(solution)/shard_map/reduce_scatter | solution.py:278
  438.4 5.5 %copy-start.2 = (f32[3584,64]{0,1:T(8,128)S(1)}, f32[3584,64]{0,1:T(8,128)}, u32[]{:S(2)}) copy-start(f32[3584,64]{0,1:T(8,128)} %all-reduce.2.cloned.1.call-done) | copy-start | bytes 2752516
Sparse Core Ops, SparseCore 0:
  20.9 148.0 all-reduce.1
Sparse Core Ops, SparseCore 1:
  40.0 163.1 reduce-scatter.1

commit v2 on v1

--- a/solution.py
+++ b/solution.py
@@ -13,18 +13,26 @@
 AHEAD = 8
 RELAY = 4
 LAG = 4
-BUFS = 4
+VMEM_BYTES = 63 * 1024 * 1024
+BUFS = 3
 
 
 def nt(a, b):
     return lax.dot_general(a, b, (((1,), (1,)), ((), ())), preferred_element_type=jnp.float32)
 
 
+def tn(a, b):
+    return lax.dot_general(a, b, (((0,), (0,)), ((), ())), preferred_element_type=jnp.float32)
+
+
 def hidden_kernel(
-    n_rs, n_seq, tile, og, w, lora_g, first, out,
-    slots, acts, part_in, part_out, staged,
-    s1s, s1r, s2s, s2r, s3s, s3r, pss, psr, axs, axr, bcs, bcr, loc, outs,
+    n_dp, n_seq, tile, og, w, first, second, kept, index, scale, count, out, first_out, second_out,
+    slots, acts, part_in, part_out, staged, stream, lora_g, terms, terms_in, sums, sums_in,
+    pieces, pieces_in, whole,
+    s1s, s1r, s2s, s2r, s3s, s3r, pss, psr, axs, axr, bcs, bcr, loc, outs, strs,
+    tss, tsr, uss, usr, vss, vsr, wss, wsr,
 ):
+    n_rs = n_dp // GROUP
     d, s = lax.axis_index("dp"), lax.axis_index("seq")
     hi, lo = d // GROUP, lax.rem(d, GROUP)
     chunks = w.shape[0] // tile
@@ -45,10 +53,12 @@
     partners = [(xor(hi, r) * GROUP + lo, s) for r in range(1, n_rs)]
     peers = [(d, xor(s, q)) for q in range(1, n_seq)]
 
+    group_peers = [(xor(d, k), s) for k in range(1, n_dp)]
+
     barrier = pltpu.get_barrier_semaphore()
-    for other in [px, pz] + partners + peers:
+    for other in group_peers + peers:
         pl.semaphore_signal(barrier, inc=1, device_id=other, device_id_type=MESH)
-    pl.semaphore_wait(barrier, 2 + len(partners) + len(peers))
+    pl.semaphore_wait(barrier, len(group_peers) + len(peers))
 
     def rows(c):
         return pl.ds(pl.multiple_of(c * tile, tile), tile)
@@ -105,9 +115,72 @@
         own_z(c).start()
         own_x(c).start()
 
-    for copy in local:
+    for copy in local[1:] + local[:1]:
         copy.start()
+
+    others = [(r, j) for j in range(GROUP) for r in range(1, n_rs)]
+
+    def streamed(at):
+        r, j = others[at]
+        return pltpu.make_async_copy(
+            og.at[:, columns(xor(hi, r), j)], stream, strs.at[at]
+        )
+
+    if others:
+        streamed(0).start()
+
+    kept_slots = index.shape[1]
+    factor = adapter_scale / tokens
+    picks = (
+        lax.broadcasted_iota(jnp.int32, (tokens, kept_slots), 0) == index[...]
+    ).astype(jnp.float32).astype(jnp.bfloat16)
+    valid = lax.broadcasted_iota(jnp.int32, (1, kept_slots), 1) < count[0]
+    weights_row = jnp.where(valid, scale[...], 0.0)
+    diagonal = lax.broadcasted_iota(jnp.int32, (kept_slots, kept_slots), 0) == (
+        lax.broadcasted_iota(jnp.int32, (kept_slots, kept_slots), 1)
+    )
+    weights = jnp.sum(jnp.where(diagonal, weights_row, 0.0), axis=1, keepdims=True)
+    kept_h = nt(kept[...], first[...])
+    scaled = weights * kept_h
+    scaled_high = scaled.astype(jnp.bfloat16)
+    scaled_low = (scaled - scaled_high.astype(jnp.float32)).astype(jnp.bfloat16)
+    cut = width // n_seq
+
+    def side(block, r, j, total):
+        at = xor(hi, r) * GROUP + xor(lo, j)
+        span = pl.ds(pl.multiple_of(at * width, width), width)
+        chosen = tn(picks, block).astype(jnp.bfloat16)
+        term = (tn(scaled_high, chosen) + tn(scaled_low, chosen)) * factor
+        for q in range(n_seq):
+            terms[q, at] = term[:, q * cut : (q + 1) * cut].astype(jnp.bfloat16)
+        return total + nt(block, second[:, span])
+
+    def gather_terms(q):
+        return remote(terms.at[xor(s, q)], terms_in.at[q - 1], tss.at[q - 1], tsr.at[q - 1], peers[q - 1])
+
+    def reduce_terms(k):
+        return remote(sums.at[xor(d, k)], sums_in.at[k - 1], uss.at[k - 1], usr.at[k - 1], group_peers[k - 1])
+
+    def reduce_first(k):
+        return remote(pieces.at[xor(d, k)], pieces_in.at[k - 1], vss.at[k - 1], vsr.at[k - 1], group_peers[k - 1])
+
+    def gather_first(k):
+        return remote(whole.at[d], whole.at[d], wss.at[k - 1], wsr.at[k - 1], group_peers[k - 1])
+
+    def landed_first(k):
+        at = xor(d, k)
+        return remote(whole.at[at], whole.at[at], wss.at[k - 1], wsr.at[k - 1], group_peers[k - 1])
+
+    total = jnp.zeros(lora_g.shape, jnp.float32)
     for j in range(GROUP):
+        local[1 + j].wait()
+        total = side(acts[0, j], 0, j, total)
+        for r in range(1, n_rs):
+            at = others.index((r, j))
+            streamed(at).wait()
+            total = side(stream[...], r, j, total)
+            if at + 1 < len(others):
+                streamed(at + 1).start()
         for r in range(n_rs - 1):
             exchange(r, j).wait_recv()
             for q in range(n_seq - 1):
@@ -115,8 +188,16 @@
         if j < relayed:
             own_z(j).wait_recv()
             relay(j).start()
-    for copy in local:
-        copy.wait()
+    for q in range(1, n_seq):
+        gather_terms(q).start()
+    lora_g[...] = total.astype(jnp.bfloat16)
+    w_rows = (weights * tn(picks, lora_g[...])).astype(jnp.bfloat16)
+    half = w.shape[0] // 2
+    both = jnp.concatenate([tn(kept[:, :half], w_rows), tn(kept[:, half:], w_rows)], axis=1)
+    pieces[...] = (both * factor).astype(jnp.bfloat16).reshape(pieces.shape)
+    for k in range(1, n_dp):
+        reduce_first(k).start()
+    local[0].wait()
     for j in range(GROUP):
         for r in range(n_rs - 1):
             for q in range(n_seq - 1):
@@ -138,6 +219,38 @@
 
     @pl.loop(0, chunks + lag)
     def _(c):
+        @pl.when(c == chunks // 4)
+        def _():
+            for q in range(1, n_seq):
+                gather_terms(q).wait_recv()
+            for b in range(n_dp):
+                part = terms[s, b].astype(jnp.float32)
+                for q in range(1, n_seq):
+                    part += terms_in[q - 1, b].astype(jnp.float32)
+                sums[b] = part.astype(jnp.bfloat16)
+            for k in range(1, n_dp):
+                reduce_terms(k).start()
+                reduce_first(k).wait_recv()
+            part = pieces[d].astype(jnp.float32)
+            for k in range(1, n_dp):
+                part += pieces_in[k - 1].astype(jnp.float32)
+            whole[d] = part.astype(jnp.bfloat16)
+            for k in range(1, n_dp):
+                gather_first(k).start()
+
+        @pl.when(c == chunks // 2)
+        def _():
+            for k in range(1, n_dp):
+                reduce_terms(k).wait_recv()
+                landed_first(k).wait_recv()
+            part = sums[d].astype(jnp.float32)
+            for k in range(1, n_dp):
+                part += sums_in[k - 1].astype(jnp.float32)
+            second_out[...] = part
+            values = whole[...].astype(jnp.float32).reshape(half, whole.shape[2]).T
+            first_out[:, :half] = values[: first.shape[0]]
+            first_out[:, half:] = values[first.shape[0] :]
+
         @pl.when(c + ahead < chunks)
         def _():
             own_z(c + ahead).start()
@@ -162,7 +275,9 @@
         @pl.when(c >= lag)
         def _():
             f = c - lag
-            total = product(0, f) + adapter_scale * nt(lora_g[...], first[rows(f)])
+            total = product(0, f) + adapter_scale * jnp.dot(
+                lora_g[...], first[:, rows(f)], preferred_element_type=jnp.float32
+            )
             for r in range(n_rs - 1):
                 partial(r, f).wait_recv()
                 total += part_in[r, f].astype(jnp.float32)
@@ -182,6 +297,12 @@
         own_z(c).wait_send()
         relay(c).wait_send()
 
+    for q in range(1, n_seq):
+        gather_terms(q).wait_send()
+    for k in range(1, n_dp):
+        reduce_terms(k).wait_send()
+        reduce_first(k).wait_send()
+        gather_first(k).wait_send()
     for r in range(n_rs - 1):
         for f in range(max(chunks - BUFS, 0), chunks):
             partial(r, f).wait_send()
@@ -191,94 +312,62 @@
                 spread(r, j, q).wait_send()
 
 
-def hidden(n_dp, n_seq, og, w, lora_g, first):
+def on_device(n_dp, n_seq, og, w, first, second, kept, index, count, scale):
     tokens, hidden_rows, width = og.shape[0], w.shape[0], w.shape[1]
+    rank = second.shape[0]
     n_rs = n_dp // GROUP
     tile = next(t for t in (256, 128) if hidden_rows % t == 0)
     chunks = hidden_rows // tile
+    cut = second.shape[1] // (n_dp * n_seq)
+    piece = hidden_rows // (2 * n_dp)
     dma = pltpu.SemaphoreType.DMA
     bf16 = jnp.bfloat16
     others = n_rs - 1
-    return pl.pallas_call(
-        functools.partial(hidden_kernel, n_rs, n_seq, tile),
-        out_shape=jax.ShapeDtypeStruct((tokens, hidden_rows), bf16),
-        in_specs=[
-            pl.BlockSpec(memory_space=pl.ANY),
-            pl.BlockSpec(memory_space=pl.ANY),
-            pl.BlockSpec(memory_space=pltpu.VMEM),
-            pl.BlockSpec(memory_space=pltpu.VMEM),
-        ],
-        out_specs=pl.BlockSpec(memory_space=pl.ANY),
+    anywhere = pl.BlockSpec(memory_space=pl.ANY)
+    vmem = pl.BlockSpec(memory_space=pltpu.VMEM)
+    smem = pl.BlockSpec(memory_space=pltpu.SMEM)
+    hidden_gradient, first_gradient, second_gradient = pl.pallas_call(
+        functools.partial(hidden_kernel, n_dp, n_seq, tile),
+        out_shape=(
+            jax.ShapeDtypeStruct((tokens, hidden_rows), bf16),
+            jax.ShapeDtypeStruct((rank, hidden_rows), jnp.float32),
+            jax.ShapeDtypeStruct((rank, cut), jnp.float32),
+        ),
+        in_specs=[anywhere, anywhere, vmem, vmem, vmem, vmem, vmem, smem],
+        out_specs=(anywhere, vmem, vmem),
         scratch_shapes=[
             pltpu.VMEM((GROUP, hidden_rows, width), bf16),
             pltpu.VMEM((n_rs, GROUP, tokens, width), bf16),
             pltpu.VMEM((others, chunks, tokens, tile), bf16),
             pltpu.VMEM((others, BUFS, tokens, tile), bf16),
             pltpu.VMEM((2, tokens, tile), bf16),
+            pltpu.VMEM((tokens, width), bf16),
+            pltpu.VMEM((tokens, rank), bf16),
+            pltpu.VMEM((n_seq, n_dp, rank, cut), bf16),
+            pltpu.VMEM((n_seq - 1, n_dp, rank, cut), bf16),
+            pltpu.VMEM((n_dp, rank, cut), bf16),
+            pltpu.VMEM((n_dp - 1, rank, cut), bf16),
+            pltpu.VMEM((n_dp, piece, 2 * rank), bf16),
+            pltpu.VMEM((n_dp - 1, piece, 2 * rank), bf16),
+            pltpu.VMEM((n_dp, piece, 2 * rank), bf16),
             dma((chunks,)), dma((chunks,)), dma((chunks,)),
             dma((chunks,)), dma((chunks,)), dma((chunks,)),
             dma((others, chunks)), dma((others, chunks)),
             dma((others, GROUP)), dma((others, GROUP)),
             dma((others, GROUP, n_seq - 1)), dma((others, GROUP, n_seq - 1)),
-            dma((GROUP + 1,)), dma((2,)),
+            dma((GROUP + 1,)), dma((2,)), dma((others * GROUP,)),
+            dma((n_seq - 1,)), dma((n_seq - 1,)), dma((n_dp - 1,)), dma((n_dp - 1,)),
+            dma((n_dp - 1,)), dma((n_dp - 1,)), dma((n_dp - 1,)), dma((n_dp - 1,)),
         ],
         compiler_params=pltpu.CompilerParams(
-            collective_id=0, has_side_effects=True, vmem_limit_bytes=62 * 1024 * 1024
+            collective_id=0, has_side_effects=True, vmem_limit_bytes=VMEM_BYTES
         ),
         cost_estimate=pl.CostEstimate(
             flops=2 * tokens * hidden_rows * width * n_dp,
             bytes_accessed=og.size * 2 + w.size * 2 * GROUP, transcendentals=0,
         ),
-    )(og, w, lora_g, first)
-
-
-def on_device(
-    n_dp,
-    n_seq,
-    output_gradient,
-    frozen_down_weight,
-    adapter_first_factor,
-    adapter_second_factor,
-    kept_hidden_rows,
-    kept_row_index,
-    kept_row_count,
-    kept_row_scale,
-):
-    contract_dims = (((1,), (1,)), ((), ()))
-    first_factor_out = (((0,), (0,)), ((), ()))
-    token_rows = output_gradient.shape[0]
-    adapter_gradient = lax.dot_general(
-        output_gradient, adapter_second_factor, contract_dims, preferred_element_type=jnp.float32
-    ).astype(jnp.bfloat16)
-    hidden_gradient = hidden(
-        n_dp, n_seq, output_gradient, frozen_down_weight, adapter_gradient, adapter_first_factor
-    )
-    slots = kept_row_index.shape[0]
-    valid = (jnp.arange(slots, dtype=jnp.int32) < kept_row_count[0]).astype(jnp.float32)
-    weight_rows = kept_row_scale * valid
-    gradient_kept_rows = jnp.take(adapter_gradient, kept_row_index, axis=0)
-    w_rows = (weight_rows[:, None] * gradient_kept_rows.astype(jnp.float32)).astype(jnp.bfloat16)
-    part_a = lax.dot_general(
-        kept_hidden_rows, w_rows, first_factor_out, preferred_element_type=jnp.float32
-    ) * (adapter_scale / token_rows)
-    first_factor_gradient = lax.psum(part_a, "dp")
-    output_gradient_kept = jnp.take(output_gradient, kept_row_index, axis=0)
-    partial_hidden_gradient = jnp.dot(
-        kept_hidden_rows, adapter_first_factor, preferred_element_type=jnp.float32
-    )
-    scaled_gradient_rows = weight_rows[:, None] * partial_hidden_gradient
-    chosen = output_gradient_kept.astype(jnp.float32)
-    term_b = lax.dot_general(
-        scaled_gradient_rows,
-        chosen,
-        first_factor_out,
-        precision=lax.Precision.HIGHEST,
-        preferred_element_type=jnp.float32,
-    ) * (adapter_scale / token_rows)
-    second_factor_gradient = lax.psum_scatter(
-        term_b, ("dp", "seq"), scatter_dimension=1, tiled=True
-    )
-    return (hidden_gradient, first_factor_gradient, second_factor_gradient)
+    )(og, w, first.T, second, kept, index.reshape(1, -1), scale.reshape(1, -1), count)
+    return hidden_gradient, first_gradient.T, second_gradient
 
 
 def solution(mesh):

time: 452 us -> 401 us (0.89)
  matrix products: 15.4 us -> 0 us
  between operations: 16.2 us -> 1.3 us
  local copies, waits for them, and re-layouts: 21.6 us -> 7 us
  Pallas kernels: 397 us -> 392 us
    dot_general x4 -> x0, matrix products: 15.4 us -> none  [the longest x1 8.21 us: on_device(): lax.dot_general(output_gradient, adapter_second_factor, contract_dims, pr...]
    gather x2 -> x0, local copies, waits for them, and re-layouts: 14 us -> none  [the longest x1 13.2 us: on_device(): output_gradient_kept = jnp.take(output_gradient, kept_row_index, axis=0)]
    pallas_call x1, Pallas kernels: 397 us -> 392 us  [on_device(): pl.pallas_call(functools.partial(hidden_kernel, n_dp, n_seq, tile), out_s...]
  transfers between devices with their start and end apart: 2 -> 0, of which waited for: 0 -> 0; matrix products, arithmetic and copies ran while one was open for 4% -> 0% of each run, Pallas kernels for 88% -> 0%
where the time goes in v2:
time: 401 us
  Pallas kernels  392 us (98%)
  local copies, waits for them, and re-layouts  7 us (2%)
    pallas_call x1, Pallas kernels, on_device(): pl.pallas_call(functools.partial(hidden_kernel, n_dp, n_seq, tile), out_s...  392 us

profile of v2, /device:TPU:0, one launch (start us, length us, event | category | flops | bytes accessed | tf_op | source)
XLA Modules:
  0.0 400.7 jit_solution(6664922796400831521)
XLA Ops:
  1.3 392.4 %shard_map.103 = (bf16[768,3584]{1,0:T(8,128)(2,1)}, f32[64,3584]{1,0:T(8,128)}, f32[64,256]{1,0:T(8,128)}) custom-call(bf16[768,8192]{1,0:T(8,128)(2,1)} %og.1, bf16[3584,1024]{1,0:T(8,128)(2,1)} %w.1, bf16[64,3584]{1,0:T(8,128)(2,1)} %bitcast.5, bf16[64,8192]{1,0:T(8,128)(2,1)} %second.1, bf16[192,3584]{1,0:T(8,128)(2,1)} %kept.1, s32[1,192]{1,0:T(1,128)} %bitcast.6, ...), custom_call_target="tpu_custom_call" | custom-call | flops 45097156608 | bytes 41943040 | tf_op jit(solution)/shard_map/pallas_call | solution.py:329
  393.7 0.0 copy-start
  393.7 0.0 copy-start.1
  393.7 5.4 %copy.15 = bf16[768,3584]{1,0:T(8,128)(2,1)} copy(bf16[768,3584]{1,0:T(8,128)(2,1)} %get-tuple-element.12) | data formatting | bytes 11010048
  399.2 0.0 copy-done
  399.2 0.9 copy.16
  400.1 0.0 copy-done.1
  400.1 0.6 copy.17
Async XLA Ops:
  393.7 5.5 %copy-start = (f32[64,3584]{1,0:T(8,128)S(1)}, f32[64,3584]{1,0:T(8,128)}, u32[]{:S(2)}) copy-start(f32[64,3584]{1,0:T(8,128)} %get-tuple-element.7) | copy-start | bytes 2752516
  393.7 6.4 %copy-start.1 = (f32[64,256]{1,0:T(8,128)S(1)}, f32[64,256]{1,0:T(8,128)}, u32[]{:S(2)}) copy-start(f32[64,256]{1,0:T(8,128)} %get-tuple-element.14) | copy-start | bytes 196612
